TPU v7x, 32 devices: a whole 2x2x4 slice. The times are simulated.
32 devices in a mesh: dp: 8 (over z, core), help: 4 (over y, x).
Axes of the slice: x: 2, y: 2, z: 4, core: 2. Of those that a mesh axis runs over, the one named last changes fastest.
Arguments:
- queries: bfloat16 [8192, 16, 128], P(('dp', 'help')), may hold values from -48 to 48
- keys_values: bfloat16 [8192, 4, 256], P(('dp', 'help')), may hold values from -4 to 4
- segment_ids: int32 [8, 1024], P('dp', 'help'), may hold values from 0 to 3, never falling along the last dimension, each value on 1 to 512 neighbouring positions
- residual: bfloat16 [8192, 4096], P(('dp', 'help')), may hold values from -3 to 3
- out_weight: bfloat16 [2048, 4096], P(None, 'dp'), may hold values from -1 to 1
Outputs:
- layer_out: bfloat16 [8192, 4096], P(('dp', 'help'))
All inputs are finite; a program needn't handle non-finite values.
Results may differ from a plain program's by a relative error of at most 0.0085.
Values may be sent and summed in bfloat16 or wider, within the bound.
A program may use at most 128 MiB of HBM per device.

v0:
```python
import math

import jax
import jax.numpy as jnp
from jax import lax
from jax.sharding import PartitionSpec as P

masked_score = -1e30


def attend_block(
    states, block_queries, block_vals, key_pos, key_seg, query_pos, query_seg, score_scale
):
    maxima, totals, running = states
    head_dim = block_queries.shape[-1]
    keys = block_vals[..., :head_dim]
    values = block_vals[..., head_dim:]
    scores = (
        jnp.einsum("qhgd,thd->hgqt", block_queries, keys, preferred_element_type=jnp.float32)
        * score_scale
    )
    allowed = (key_pos[None, :] <= query_pos[:, None]) & (key_seg[None, :] == query_seg[:, None])
    scores = jnp.where(allowed, scores, masked_score)
    new_max = jnp.maximum(maxima, jnp.max(scores, axis=-1))
    weights = jnp.where(allowed, jnp.exp(scores - new_max[..., None]), 0.0)
    factor = jnp.exp(maxima - new_max)
    totals = totals * factor + jnp.sum(weights, axis=-1)
    mixed = jnp.einsum(
        "hgqt,thd->qhgd", weights.astype(jnp.bfloat16), values, preferred_element_type=jnp.float32
    )
    running = running * jnp.transpose(factor, (2, 0, 1))[..., None] + mixed
    return (new_max, totals, running)


def start_state(rows_count, heads_kv, group_size, head_dim):
    maxima = jnp.full((heads_kv, group_size, rows_count), masked_score, jnp.float32)
    totals = jnp.zeros((heads_kv, group_size, rows_count), jnp.float32)
    running = jnp.zeros((rows_count, heads_kv, group_size, head_dim), jnp.float32)
    return (maxima, totals, running)


def finish(states):
    maxima, totals, running = states
    return (running / jnp.transpose(totals, (2, 0, 1))[..., None]).astype(jnp.bfloat16)


def heads_attention(queries, keys_values, seg_local):
    local_rows, heads, head_dim = queries.shape
    heads_kv = keys_values.shape[1]
    group_size = heads // heads_kv
    score_scale = 1.0 / math.sqrt(head_dim)
    repeated = jnp.repeat(keys_values, group_size, axis=1)
    row_queries, row_keys = (
        lax.all_to_all(queries, "help", split_axis=1, concat_axis=0, tiled=True),
        lax.all_to_all(repeated, "help", split_axis=1, concat_axis=0, tiled=True),
    )
    row_segments = lax.all_gather(seg_local, "help", axis=0, tiled=True)
    row_length = row_queries.shape[0]
    heads_here = row_queries.shape[1]
    block_rows = min(512, row_length)
    query_blocks = row_length // block_rows

    def one_block(block_index):
        query_start = block_index * block_rows
        block_queries = lax.dynamic_slice_in_dim(row_queries, query_start, block_rows, 0)
        block_queries = block_queries.reshape(block_rows, heads_here, 1, head_dim)
        query_pos = query_start + jnp.arange(block_rows, dtype=jnp.int32)
        query_seg = lax.dynamic_slice_in_dim(row_segments, query_start, block_rows, 0)
        first_key = jnp.sum((row_segments < query_seg[0]).astype(jnp.int32))
        lowest = first_key // block_rows

        def visit(key_block, states):
            key_start = key_block * block_rows
            block_vals = lax.dynamic_slice_in_dim(row_keys, key_start, block_rows, 0)
            block_seg = lax.dynamic_slice_in_dim(row_segments, key_start, block_rows, 0)
            key_pos = key_start + jnp.arange(block_rows, dtype=jnp.int32)
            return attend_block(
                states,
                block_queries,
                block_vals,
                key_pos,
                block_seg,
                query_pos,
                query_seg,
                score_scale,
            )

        initial = start_state(block_rows, heads_here, 1, head_dim)
        states = lax.fori_loop(lowest, block_index + 1, visit, initial)
        return finish(states).reshape(block_rows, heads_here, head_dim)

    row_output = lax.map(one_block, jnp.arange(query_blocks, dtype=jnp.int32))
    row_output = row_output.reshape(row_length, heads_here, head_dim)
    returned = lax.all_to_all(row_output, "help", split_axis=0, concat_axis=1, tiled=True)
    return returned.reshape(local_rows, heads * head_dim)


def on_device(queries, keys_values, segment_ids, residual, out_weight):
    local_rows = queries.shape[0]
    seg_local = segment_ids.reshape(local_rows)
    attended = heads_attention(queries, keys_values, seg_local)
    summed = jnp.dot(
        attended,
        lax.all_gather(out_weight, "dp", axis=1, tiled=True),
        preferred_element_type=jnp.float32,
    )
    return (residual.astype(jnp.float32) + summed).astype(jnp.bfloat16)


def solution(mesh):
    return jax.shard_map(
        on_device,
        mesh=mesh,
        in_specs=(
            P(("dp", "help"), None, None),
            P(("dp", "help"), None, None),
            P("dp", "help"),
            P(("dp", "help"), None),
            P(None, "dp"),
        ),
        out_specs=P(("dp", "help"), None),
        check_vma=False,
    )
```

profile of v0, /device:TPU:0, one launch (start us, length us, event | category | flops | bytes accessed | tf_op | source)
XLA Modules:
  0.0 181.5 jit_solution(8269135378736162631)
XLA Ops:
  7.3 2.5 %copy.32 = bf16[256,16,128]{2,0,1:T(8,128)(2,1)} copy(bf16[256,16,128]{2,1,0:T(8,128)(2,1)} %param.9) | data formatting | bytes 2097152 | tf_op args[0]
  9.7 5.2 %all-to-all-start = ((bf16[256,16,128]{2,0,1:T(8,128)(2,1)}), bf16[256,16,128]{2,0,1:T(8,128)(2,1)S(1)}, u32[]{:S(2)}, u32[]{:S(2)}) async-start(bf16[256,16,128]{2,0,1:T(8,128)(2,1)} %copy.32), calls=%async_computation | async-start | bytes 2097152 | tf_op jit(solution)/shard_map/all_to_all | solution.py:54
  15.0 13.6 %all-to-all-done = bf16[256,16,128]{2,0,1:T(8,128)(2,1)S(1)} async-done(((bf16[256,16,128]{2,0,1:T(8,128)(2,1)}), bf16[256,16,128]{2,0,1:T(8,128)(2,1)S(1)}, u32[]{:S(2)}, u32[]{:S(2)}) %all-to-all-start) | async-done | bytes 1048608 | tf_op jit(solution)/shard_map/all_to_all | solution.py:54
  28.5 1.5 broadcast_in_dim.33
  30.1 3.6 %all-to-all-start.1 = ((bf16[256,16,256]{2,0,1:T(8,128)(2,1)}), bf16[256,16,256]{2,0,1:T(8,128)(2,1)S(1)}, u32[]{:S(2)}, u32[]{:S(2)}) async-start(bf16[256,16,256]{2,0,1:T(8,128)(2,1)} %bitcast.11), calls=%async_computation.1 | async-start | bytes 4194304 | tf_op jit(solution)/shard_map/all_to_all | solution.py:55
  33.7 25.9 %all-gather = s32[1,1024]{1,0:T(1,128)S(1)} all-gather(s32[1,256]{1,0:T(1,128)S(1)} %copy-done.3), channel_id=2, replica_groups=mesh['dp'=8,'help'=4] {'help'}, dimensions={1}, use_global_device_ids=true | all-gather | bytes 5120 | tf_op jit(solution)/shard_map/all_gather | solution.py:57
  60.7 1.3 copy-done.1
  62.0 1.8 copy.35
  63.8 50.2 %while.40 = (s32[]{:T(128)}, bf16[2,512,4,128]{3,1,0,2:T(8,128)(2,1)}, s32[2]{0:T(128)S(1)}, s32[1024]{0:T(1024)S(1)}, bf16[1024,4,128]{2,0,1:T(8,128)(2,1)}, /*...) while((s32[]{:T(128)}, ...), condition=%wide.region_6.7_spmd, body=%wide.region_0.6_spmd.sunk | while | flops 552347648 | bytes 40027436 | solution.py:92
  65.6 1.2 convert_reduce_fusion.2
  69.6 1.1 dynamic-slice_bitcast_fusion.2
  71.4 1.1 broadcast.53
  72.5 9.2 %while.41 = (s32[]{:T(128)}, f32[4,1,512]{2,0,1:T(4,128)S(1)}, f32[4,1,512]{2,0,1:T(4,128)S(1)}, f32[512,4,1,128]{0,3,1,2:T(8,128)}, s32[]{:T(128)}, /*index=5*/...) while((s32[]{:T(128)}, f32[4,1,512]{2,0,1:T(4,128)S(1)}, ...), condition=%wide.region_5.5_spmd.clone, body=%wide.region_2.4_spmd.clone.sunk | while | flops 551820288 | bytes 34226424 | solution.py:89
  72.9 2.8 %fusion.39 = (f32[4,512]{1,0:T(4,128)S(1)}, f32[4,512,512]{2,1,0:T(8,128)}) fusion(pred[512,512]{0,1:T(8,128)(4,1)S(1)} %compare_and_fusion.2, bf16[512,4,1,128]{3,0,1,2:T(8,128)(2,1)S(1)} %get-tuple-element.373, bf16[1024,4,256]{2,0,1:T(8,128)(2,1)S(1)} %get-tuple-element.372, s32[]{:T(128)S(6)} %select_n.72), kind=kOutput, calls=%fused_computation.3.clone.1 | convolution fusion | flops 271579136 | bytes 5513220 | tf_op jit(solution)/shard_map/while/body/eval_jaxpr/while/body/qhgd,thd->hgqt/dot_general | solution.py:19
  75.7 5.0 %fusion.42 = f32[512,4,1,128]{0,3,1,2:T(8,128)} fusion(f32[4,512,512]{2,1,0:T(8,128)} %get-tuple-element.333, f32[4,512]{1,0:T(4,128)S(1)} %bitcast.105, pred[512,512]{0,1:T(8,128)(4,1)S(1)} %compare_and_fusion.2, f32[512,4,1,128]{0,3,1,2:T(8,128)} %get-tuple-element.353, bf16[1024,4,256]{2,0,1:T(8,128)(2,1)S(1)} %get-tuple-element.372, ...), kind=kOutput, calls=%fused_computation.10.clone.1 | convolution fusion | flops 274202624 | bytes 7094280 | tf_op jit(solution)/shard_map/while/body/eval_jaxpr/while/body/hgqt,thd->qhgd/dot_general | solution.py:28
  80.6 1.0 fusion.41
  81.7 1.4 fusion.36
  86.1 1.2 convert_reduce_fusion.2
  90.1 1.1 dynamic-slice_bitcast_fusion.2
  91.9 1.1 broadcast.53
  93.0 18.6 %while.41 = (s32[]{:T(128)}, f32[4,1,512]{2,0,1:T(4,128)S(1)}, f32[4,1,512]{2,0,1:T(4,128)S(1)}, f32[512,4,1,128]{0,3,1,2:T(8,128)}, s32[]{:T(128)}, /*index=5*/...) while((s32[]{:T(128)}, f32[4,1,512]{2,0,1:T(4,128)S(1)}, ...), condition=%wide.region_5.5_spmd.clone, body=%wide.region_2.4_spmd.clone.sunk | while | flops 551820288 | bytes 34226424 | solution.py:89
  93.3 2.8 %fusion.39 = (f32[4,512]{1,0:T(4,128)S(1)}, f32[4,512,512]{2,1,0:T(8,128)}) fusion(pred[512,512]{0,1:T(8,128)(4,1)S(1)} %compare_and_fusion.2, bf16[512,4,1,128]{3,0,1,2:T(8,128)(2,1)S(1)} %get-tuple-element.373, bf16[1024,4,256]{2,0,1:T(8,128)(2,1)S(1)} %get-tuple-element.372, s32[]{:T(128)S(6)} %select_n.72), kind=kOutput, calls=%fused_computation.3.clone.1 | convolution fusion | flops 271579136 | bytes 5513220 | tf_op jit(solution)/shard_map/while/body/eval_jaxpr/while/body/qhgd,thd->hgqt/dot_general | solution.py:19
  96.2 5.0 %fusion.42 = f32[512,4,1,128]{0,3,1,2:T(8,128)} fusion(f32[4,512,512]{2,1,0:T(8,128)} %get-tuple-element.333, f32[4,512]{1,0:T(4,128)S(1)} %bitcast.105, pred[512,512]{0,1:T(8,128)(4,1)S(1)} %compare_and_fusion.2, f32[512,4,1,128]{0,3,1,2:T(8,128)} %get-tuple-element.353, bf16[1024,4,256]{2,0,1:T(8,128)(2,1)S(1)} %get-tuple-element.372, ...), kind=kOutput, calls=%fused_computation.10.clone.1 | convolution fusion | flops 274202624 | bytes 7094280 | tf_op jit(solution)/shard_map/while/body/eval_jaxpr/while/body/hgqt,thd->qhgd/dot_general | solution.py:28
  101.2 1.0 fusion.41
  102.7 2.8 %fusion.39 = (f32[4,512]{1,0:T(4,128)S(1)}, f32[4,512,512]{2,1,0:T(8,128)}) fusion(pred[512,512]{0,1:T(8,128)(4,1)S(1)} %compare_and_fusion.2, bf16[512,4,1,128]{3,0,1,2:T(8,128)(2,1)S(1)} %get-tuple-element.373, bf16[1024,4,256]{2,0,1:T(8,128)(2,1)S(1)} %get-tuple-element.372, s32[]{:T(128)S(6)} %select_n.72), kind=kOutput, calls=%fused_computation.3.clone.1 | convolution fusion | flops 271579136 | bytes 5513220 | tf_op jit(solution)/shard_map/while/body/eval_jaxpr/while/body/qhgd,thd->hgqt/dot_general | solution.py:19
  105.5 5.0 %fusion.42 = f32[512,4,1,128]{0,3,1,2:T(8,128)} fusion(f32[4,512,512]{2,1,0:T(8,128)} %get-tuple-element.333, f32[4,512]{1,0:T(4,128)S(1)} %bitcast.105, pred[512,512]{0,1:T(8,128)(4,1)S(1)} %compare_and_fusion.2, f32[512,4,1,128]{0,3,1,2:T(8,128)} %get-tuple-element.353, bf16[1024,4,256]{2,0,1:T(8,128)(2,1)S(1)} %get-tuple-element.372, ...), kind=kOutput, calls=%fused_computation.10.clone.1 | convolution fusion | flops 274202624 | bytes 7094280 | tf_op jit(solution)/shard_map/while/body/eval_jaxpr/while/body/hgqt,thd->qhgd/dot_general | solution.py:28
  110.4 1.0 fusion.41
  111.5 1.4 fusion.36
  114.1 2.0 %copy.37 = bf16[1024,4,128]{2,1,0:T(4,128)(2,1)S(1)} copy(bf16[1024,4,128]{2,0,1:T(8,128)(2,1)} %bitcast.114) | data formatting | bytes 2097152 | tf_op jit(solution)/shard_map/reshape | solution.py:93
  116.1 14.0 %all_to_all.51 = bf16[1024,4,128]{2,1,0:T(4,128)(2,1)S(1)} all-to-all(bf16[1024,4,128]{2,1,0:T(4,128)(2,1)S(1)} %copy.37), channel_id=1, replica_groups=mesh['dp'=8,'help'=4] {'help'}, dimensions={0} | all-to-all | bytes 2097152 | tf_op jit(solution)/shard_map/all_to_all | solution.py:94
  130.8 32.0 %all-gather.3.cloned.1.call-done = bf16[2048,4096]{1,0:T(8,128)(2,1)} async-done(((bf16[2048,512]{1,0:T(8,128)(2,1)}), bf16[2048,4096]{1,0:T(8,128)(2,1)}) %all-gather.3.cloned.1.call-update) | async-done | bytes 16777232 | tf_op jit(solution)/shard_map/all_gather | solution.py:104
  162.8 11.8 %fusion.26 = bf16[256,4096]{1,0:T(8,128)(2,1)} fusion(bf16[256,2048]{0,1:T(8,128)(2,1)S(1)} %bitcast.112, bf16[2048,4096]{1,0:T(8,128)(2,1)} %all-gather.3.cloned.1.call-done, bf16[256,4096]{1,0:T(8,128)(2,1)} %param.12), kind=kOutput, calls=%fused_computation.33 | convolution fusion | flops 4298113024 | bytes 22020096 | tf_op jit(solution)/shard_map/dot_general | solution.py:102
  (52 shorter events, 8.3 us)
Async XLA Ops:
  6.5 8.4 %copy-start.2 = (bf16[256,4,256]{2,1,0:T(4,128)(2,1)S(1)}, bf16[256,4,256]{2,1,0:T(4,128)(2,1)}, u32[]{:S(2)}) copy-start(bf16[256,4,256]{2,1,0:T(4,128)(2,1)} %param.10) | copy-start | bytes 1572868
  6.5 156.3 %all-gather.3.cloned.1.call-start = ((), (), s32[]{:S(2)}) async-start(), calls=%async_computation.3 | async-start | bytes 18874368 | tf_op jit(solution)/shard_map/all_gather | solution.py:104
  9.7 18.8 %all-to-all-start = ((bf16[256,16,128]{2,0,1:T(8,128)(2,1)}), bf16[256,16,128]{2,0,1:T(8,128)(2,1)S(1)}, u32[]{:S(2)}, u32[]{:S(2)}) async-start(bf16[256,16,128]{2,0,1:T(8,128)(2,1)} %copy.32), calls=%async_computation | async-start | bytes 2097152 | tf_op jit(solution)/shard_map/all_to_all | solution.py:54
  14.9 18.8 %copy-start.3 = (s32[1,256]{1,0:T(1,128)S(1)}, s32[1,256]{1,0:T(1,128)}, u32[]{:S(2)}) copy-start(s32[1,256]{1,0:T(1,128)} %param.11) | copy-start | bytes 3076
  30.1 30.6 %all-to-all-start.1 = ((bf16[256,16,256]{2,0,1:T(8,128)(2,1)}), bf16[256,16,256]{2,0,1:T(8,128)(2,1)S(1)}, u32[]{:S(2)}, u32[]{:S(2)}) async-start(bf16[256,16,256]{2,0,1:T(8,128)(2,1)} %bitcast.11), calls=%async_computation.1 | async-start | bytes 4194304 | tf_op jit(solution)/shard_map/all_to_all | solution.py:55
  60.7 1.3 copy-start.1
  75.7 5.0 %copy-start = (f32[4,512,512]{2,1,0:T(8,128)S(1)}, f32[4,512,512]{2,1,0:T(8,128)}, u32[]{:S(2)}) copy-start(f32[4,512,512]{2,1,0:T(8,128)} %get-tuple-element.333) | copy-start | bytes 12582916 | tf_op jit(solution)/shard_map/while/body/eval_jaxpr/while
  96.1 5.0 %copy-start = (f32[4,512,512]{2,1,0:T(8,128)S(1)}, f32[4,512,512]{2,1,0:T(8,128)}, u32[]{:S(2)}) copy-start(f32[4,512,512]{2,1,0:T(8,128)} %get-tuple-element.333) | copy-start | bytes 12582916 | tf_op jit(solution)/shard_map/while/body/eval_jaxpr/while
  105.5 5.0 %copy-start = (f32[4,512,512]{2,1,0:T(8,128)S(1)}, f32[4,512,512]{2,1,0:T(8,128)}, u32[]{:S(2)}) copy-start(f32[4,512,512]{2,1,0:T(8,128)} %get-tuple-element.333) | copy-start | bytes 12582916 | tf_op jit(solution)/shard_map/while/body/eval_jaxpr/while
Sparse Core Ops, SparseCore 0:
  9.0 153.7 all-gather.2
where the time goes:
time: 182 us; the launch traced here: 181 us
  waiting for transfers between devices  46.3 us (25%)
  blocking collectives  39.9 us (22%)
  matrix products  35.2 us (19%)
  local copies, waits for them, and re-layouts  20.2 us (11%)
  between operations  13.5 us (7%)
  other arithmetic  9.28 us (5%)
  starting transfers between devices  8.78 us (5%)
  loops' own time  8.36 us (5%)
    all_gather x1, waiting for transfers between devices, on_device(): lax.all_gather(out_weight, 'dp', axis=1, tiled=True)  32 us
    all_gather x1, blocking collectives, heads_attention(): row_segments = lax.all_gather(seg_local, 'help', axis=0, tiled=True)  25.9 us
    dot_general x3, matrix products, attend_block(): jnp.einsum('hgqt,thd->qhgd', weights.astype(jnp.bfloat16), values, prefer...  14.9 us
    all_to_all x1, blocking collectives, heads_attention(): lax.all_to_all(row_output, 'help', split_axis=0, concat_axis=1, tiled=True)  14 us
    all_to_all x1, waiting for transfers between devices, heads_attention(): lax.all_to_all(queries, 'help', split_axis=1, concat_axis=0, tiled=True)  13.6 us
    dot_general x1, matrix products, on_device(): jnp.dot(attended, lax.all_gather(out_weight, 'dp', axis=1, tiled=True), p...  11.8 us
    dot_general x3, matrix products, attend_block(): jnp.einsum('qhgd,thd->hgqt', block_queries, keys, preferred_element_type=...  8.41 us
    another operation x1, loops' own time, heads_attention(): row_output = lax.map(one_block, jnp.arange(query_blocks, dtype=jnp.int32))  8.23 us
  transfers between devices with their start and end apart: 3, of which 2 were waited for; matrix products, arithmetic and copies ran while one was open for 28% of the time, Pallas kernels for 0%

commit v1 on v0

v1 whole, which is shorter than its diff:
```python
import functools
import math

import jax
import jax.numpy as jnp
from jax import lax
from jax.experimental import pallas as pl
from jax.experimental.pallas import tpu as pltpu
from jax.sharding import PartitionSpec as P

MESH = pl.DeviceIdType.MESH
masked_score = -1e30


def kernel(
    dims,
    q_ref,
    kv_ref,
    segr_ref,
    segc_ref,
    res_ref,
    w_ref,
    out_ref,
    wbuf,
    kvbuf,
    segbuf,
    qbuf,
    att,
    resbuf,
    ost,
    w_recv,
    z_send,
    p_send,
    kv_recv,
    kv_send,
    seg_recv,
    seg_send,
    res_recv,
    res_send,
    att_recv,
    att_send,
    out_recv,
    out_send,
    loc,
    loc_out,
):
    nz, ny, nx, back, heads, heads_kv, hd, rows, cols, width = dims
    nh = ny * nx
    quarter = width // nh
    piece_rows = quarter // 2
    dp = lax.axis_index("dp")
    h = lax.axis_index("help")
    z, c = dp // 2, lax.rem(dp, 2)
    y, x = h // nx, lax.rem(h, nx)
    sib = (z * 2 + (1 - c), h)
    x_mates = [lax.rem(x + i, nx) for i in range(1, nx)]
    y_mates = [lax.rem(y + i, ny) for i in range(1, ny)]

    def column(zp, core):
        return pl.ds(pl.multiple_of((zp * 2 + core) * cols, cols), cols)

    def own_rows(core):
        return pl.ds(pl.multiple_of(core * rows, rows), rows)

    def piece(zp, hp, half):
        start = pl.multiple_of(hp * quarter + half * piece_rows, piece_rows)
        return wbuf.at[zp, pl.ds(start, piece_rows)]

    def remote(src, dst, ssem, rsem, dev):
        return pltpu.make_async_remote_copy(
            src_ref=src, dst_ref=dst, send_sem=ssem, recv_sem=rsem, device_id=dev, device_id_type=MESH
        )

    barrier = pltpu.get_barrier_semaphore()
    greet = functools.partial(pl.semaphore_signal, barrier, inc=1, device_id_type=MESH)
    greet(device_id=sib)
    for i in range(1, nh):
        greet(device_id=(dp, lax.rem(h + i, nh)))

    @pl.when(z > 0)
    def _():
        greet(device_id=(dp - 2, h))

    @pl.when(z < nz - 1)
    def _():
        greet(device_id=(dp + 2, h))

    pl.semaphore_wait(
        barrier, nh + jnp.where(z > 0, 1, 0) + jnp.where(z < nz - 1, 1, 0)
    )

    def z_copy(src, zp, half, way, step):
        dev = (dp + 2, h) if way == 0 else (dp - 2, h)
        return remote(src, piece(zp, h, half), z_send.at[way, step, half], w_recv.at[zp, h, half], dev)

    def own_piece(half):
        start = pl.multiple_of(h * quarter + half * piece_rows, piece_rows)
        return w_ref.at[pl.ds(start, piece_rows)]

    for half in range(2):

        @pl.when(z < nz - 1)
        def _(half=half):
            z_copy(own_piece(half), z, half, 0, 0).start()

        @pl.when(z > 0)
        def _(half=half):
            z_copy(own_piece(half), z, half, 1, 0).start()

    def seg_copy(j):
        return remote(segr_ref, segbuf.at[j], seg_send.at[j], seg_recv.at[j], (dp, lax.rem(h + j, nh)))

    def kv_copy(j, g):
        return remote(
            kv_ref.at[g], kvbuf.at[j, g], kv_send.at[j, g], kv_recv.at[j, g], (dp, lax.rem(h + j, nh))
        )

    for j in range(1, back + 1):

        @pl.when(h + j < nh)
        def _(j=j):
            seg_copy(j).start()

    for g in range(heads_kv):
        for j in range(1, back + 1):

            @pl.when(h + j < nh)
            def _(j=j, g=g):
                kv_copy(j, g).start()

    local = [
        pltpu.make_async_copy(q_ref, qbuf, loc.at[0]),
        pltpu.make_async_copy(kv_ref, kvbuf.at[0], loc.at[1]),
        pltpu.make_async_copy(segr_ref, segbuf.at[0], loc.at[2]),
        pltpu.make_async_copy(w_ref, wbuf.at[z], loc.at[3]),
    ]
    for copy in local:
        copy.start()

    def res_copy(zp):
        return remote(
            res_ref.at[:, column(zp, 1 - c)],
            resbuf.at[zp, own_rows(c)],
            res_send.at[zp],
            res_recv.at[zp],
            sib,
        )

    def res_local(zp):
        return pltpu.make_async_copy(
            res_ref.at[:, column(zp, c)], resbuf.at[zp, own_rows(c)], loc.at[4 + zp]
        )

    for zp in range(nz):
        res_copy(zp).start()
        res_local(zp).start()

    def both_ways(step, run):
        @pl.when(z >= step)
        def _():
            run(z - step, 0)

        @pl.when(z + step < nz)
        def _():
            run(z + step, 1)

    def to_x(zp, hp, half):
        for xm in x_mates:
            remote(
                piece(zp, hp, half), piece(zp, hp, half), p_send.at[zp], w_recv.at[zp, hp, half], (dp, y * nx + xm)
            ).start()

    def to_y(zp, hp, half):
        for ym in y_mates:
            remote(
                piece(zp, hp, half), piece(zp, hp, half), p_send.at[zp], w_recv.at[zp, hp, half], (dp, ym * nx + x)
            ).start()

    def arrived(zp, hp, half):
        remote(
            piece(zp, hp, half), piece(zp, hp, half), p_send.at[zp], w_recv.at[zp, hp, half], sib
        ).wait_recv()

    def from_z(step, half):
        def run(zp, way):
            arrived(zp, h, half)

            @pl.when((z < nz - 1) if way == 0 else (z > 0))
            def _():
                z_copy(piece(zp, h, half), zp, half, way, step).start()

            to_x(zp, h, half)
            to_y(zp, h, half)

        both_ways(step, run)

    def relay(step):
        def run(zp, way):
            for xm in x_mates:
                arrived(zp, y * nx + xm, 0)
                to_y(zp, y * nx + xm, 0)
            for ym in y_mates:
                arrived(zp, ym * nx + x, 1)
                to_x(zp, ym * nx + x, 1)

        both_ways(step, run)

    scale = 1.0 / math.sqrt(hd)
    group = heads // heads_kv
    per_chunk = 2

    def attend(g, first):
        if first == 0:
            for j in range(1, back + 1):

                @pl.when(h >= j)
                def _(j=j):
                    if g == 0:
                        seg_copy(j).wait_recv()
                    kv_copy(j, g).wait_recv()

        q_seg = segc_ref[...]
        here = [g * group + first + i for i in range(per_chunk)]

        def scores(head, j, allowed):
            s = lax.dot_general(
                qbuf[head], kvbuf[j, g, :, 0:hd], (((1,), (1,)), ((), ())), preferred_element_type=jnp.float32
            )
            return jnp.where(allowed, s * scale, masked_score)

        def mix(weights, j):
            return jnp.dot(
                weights.astype(jnp.bfloat16), kvbuf[j, g, :, hd:], preferred_element_type=jnp.float32
            )

        same = q_seg == segbuf[0, 0:1, :]
        causal = lax.broadcasted_iota(jnp.int32, (rows, rows), 1) <= lax.broadcasted_iota(
            jnp.int32, (rows, rows), 0
        )
        states = []
        for head in here:
            s = scores(head, 0, same & causal)
            top = jnp.max(s, axis=-1, keepdims=True)
            weights = jnp.exp(s - top)
            states.append((top, jnp.sum(weights, axis=-1, keepdims=True), mix(weights, 0)))

        def earlier(j, states):
            allowed = q_seg == segbuf[j, 0:1, :]
            after = []
            for head, (top, total, running) in zip(here, states):
                s = scores(head, j, allowed)
                new_top = jnp.maximum(top, jnp.max(s, axis=-1, keepdims=True))
                weights = jnp.exp(s - new_top)
                factor = jnp.exp(top - new_top)
                total = total * factor + jnp.sum(weights, axis=-1, keepdims=True)
                after.append((new_top, total, running * factor + mix(weights, j)))
            return tuple(after)

        states = lax.fori_loop(1, jnp.minimum(h, back) + 1, earlier, tuple(states))
        for head, (top, total, running) in zip(here, states):
            att[own_rows(c), head * hd : (head + 1) * hd] = (running / total).astype(jnp.bfloat16)

    def att_copy(core):
        return remote(att.at[own_rows(core)], att.at[own_rows(core)], att_send, att_recv, sib)

    tile = min(256, cols)

    def out_local(zp):
        return pltpu.make_async_copy(
            ost.at[zp, own_rows(c)], out_ref.at[:, column(zp, c)], loc_out.at[zp]
        )

    def out_copy(zp, core):
        return remote(
            ost.at[zp, own_rows(1 - c)], out_ref.at[:, column(zp, core)], out_send.at[zp], out_recv.at[zp], sib
        )

    def project(zp, way):
        @pl.loop(0, cols // tile)
        def _(n):
            part = pl.ds(pl.multiple_of(n * tile, tile), tile)
            summed = jnp.dot(att[...], wbuf[zp, :, part], preferred_element_type=jnp.float32)
            ost[zp, :, part] = (resbuf[zp, :, part].astype(jnp.float32) + summed).astype(jnp.bfloat16)

        out_copy(zp, c).start()
        out_local(zp).start()

    def complete(zp):
        for xm in x_mates:
            arrived(zp, y * nx + xm, 1)
        for ym in y_mates:
            arrived(zp, ym * nx + x, 0)
        for ym in y_mates:
            for xm in x_mates:
                arrived(zp, ym * nx + xm, 0)
                arrived(zp, ym * nx + xm, 1)

    for copy in local[:3]:
        copy.wait()
    work = [
        functools.partial(attend, g, first)
        for g in range(heads_kv)
        for first in range(0, group, per_chunk)
    ]

    def compute(count):
        for _ in range(count):
            if work:
                work.pop(0)()

    compute(1)
    for step in range(1, nz):
        from_z(step, 0)
        compute(1)
        from_z(step, 1)
        compute(1)
        relay(step)
        compute(2)
        if step == 2 or nz <= 2:
            compute(len(work))
            att_copy(c).start()
            local[3].wait()
            for zp in range(nz):
                res_local(zp).wait()
                res_copy(zp).wait_recv()
            att_copy(1 - c).wait_recv()
            project(z, 0)

    for step in range(1, nz):

        def run(zp, way):
            complete(zp)
            project(zp, way)

        both_ways(step, run)

    for zp in range(nz):
        out_local(zp).wait()
        out_copy(zp, c).wait_send()
        out_copy(zp, 1 - c).wait_recv()
        res_copy(zp).wait_send()
    att_copy(c).wait_send()
    for j in range(1, back + 1):

        @pl.when(h + j < nh)
        def _(j=j):
            seg_copy(j).wait_send()
            for g in range(heads_kv):
                kv_copy(j, g).wait_send()

    for half in range(2):

        @pl.when(z < nz - 1)
        def _(half=half):
            z_copy(own_piece(half), z, half, 0, 0).wait_send()

        @pl.when(z > 0)
        def _(half=half):
            z_copy(own_piece(half), z, half, 1, 0).wait_send()

    for step in range(1, nz):

        def drain(zp, way):
            for half in range(2):

                @pl.when((z < nz - 1) if way == 0 else (z > 0))
                def _(half=half):
                    z_copy(piece(zp, h, half), zp, half, way, step).wait_send()

            if nh > 1:
                sent = wbuf.at[zp, 0 : quarter * (nh - 1)]
                pltpu.make_async_copy(sent, sent, p_send.at[zp]).wait()

        both_ways(step, drain)


def on_device(ndp, nh, queries, keys_values, segment_ids, residual, out_weight):
    rows, heads, hd = queries.shape
    heads_kv = keys_values.shape[1]
    width, cols = out_weight.shape
    nz = ndp // 2
    nx = math.isqrt(nh)
    while nh % nx:
        nx -= 1
    ny = nh // nx
    back = nh // 2
    dims = (nz, ny, nx, back, heads, heads_kv, hd, rows, cols, width)
    seg = segment_ids.reshape(rows)
    any_spec = pl.BlockSpec(memory_space=pl.ANY)
    dma = pltpu.SemaphoreType.DMA
    bf16 = jnp.bfloat16
    return pl.pallas_call(
        functools.partial(kernel, dims),
        out_shape=jax.ShapeDtypeStruct(residual.shape, bf16),
        in_specs=[any_spec, any_spec, any_spec, pl.BlockSpec(memory_space=pltpu.VMEM), any_spec, any_spec],
        out_specs=any_spec,
        scratch_shapes=[
            pltpu.VMEM((nz, width, cols), bf16),
            pltpu.VMEM((back + 1, heads_kv, rows, 2 * hd), bf16),
            pltpu.VMEM((back + 1, 8, rows), jnp.int32),
            pltpu.VMEM((heads, rows, hd), bf16),
            pltpu.VMEM((2 * rows, width), bf16),
            pltpu.VMEM((nz, 2 * rows, cols), bf16),
            pltpu.VMEM((nz, 2 * rows, cols), bf16),
            dma((nz, nh, 2)),
            dma((2, nz, 2)),
            dma((nz,)),
            dma((back + 1, heads_kv)),
            dma((back + 1, heads_kv)),
            dma((back + 1,)),
            dma((back + 1,)),
            dma((nz,)),
            dma((nz,)),
            dma,
            dma,
            dma((nz,)),
            dma((nz,)),
            dma((4 + nz,)),
            dma((nz,)),
        ],
        compiler_params=pltpu.CompilerParams(
            collective_id=0, has_side_effects=True, vmem_limit_bytes=56 * 1024 * 1024
        ),
        cost_estimate=pl.CostEstimate(flops=6 * 10**9, bytes_accessed=2 * 10**7, transcendentals=3 * 10**6),
    )(
        jnp.transpose(queries, (1, 0, 2)),
        jnp.transpose(keys_values, (1, 0, 2)),
        jnp.broadcast_to(seg[None, :], (8, rows)),
        seg[:, None],
        residual,
        out_weight,
    )


def solution(mesh):
    return jax.shard_map(
        functools.partial(on_device, mesh.shape["dp"], mesh.shape["help"]),
        mesh=mesh,
        in_specs=(
            P(("dp", "help"), None, None),
            P(("dp", "help"), None, None),
            P("dp", "help"),
            P(("dp", "help"), None),
            P(None, "dp"),
        ),
        out_specs=P(("dp", "help"), None),
        check_vma=False,
    )
```

time: 182 us -> 97.2 us (0.53)
  Pallas kernels: 0 us -> 86.7 us
  waiting for transfers between devices: 46.3 us -> 0 us
  blocking collectives: 39.9 us -> 0 us
  matrix products: 35.2 us -> 0 us
  between operations: 13.5 us -> 0.01 us
  local copies, waits for them, and re-layouts: 20.2 us -> 10.2 us
  other arithmetic: 9.28 us -> 0 us
  starting transfers between devices: 8.78 us -> 0 us
  loops' own time: 8.36 us -> 0 us
    pallas_call x0 -> x1, Pallas kernels: none -> 86.7 us  [on_device(): pl.pallas_call(functools.partial(kernel, dims), out_shape=jax.ShapeDtypeS...]
    dot_general x7 -> x0, matrix products: 35.2 us -> none  [the longest x3 14.9 us: attend_block(): jnp.einsum('hgqt,thd->qhgd', weights.astype(jnp.bfloat16), values, prefer...]
    all_gather x1 -> x0, waiting for transfers between devices: 32 us -> none  [on_device(): lax.all_gather(out_weight, 'dp', axis=1, tiled=True)]
    all_gather x1 -> x0, blocking collectives: 25.9 us -> none  [heads_attention(): row_segments = lax.all_gather(seg_local, 'help', axis=0, tiled=True)]
    all_to_all x1 -> x0, blocking collectives: 14 us -> none  [heads_attention(): lax.all_to_all(row_output, 'help', split_axis=0, concat_axis=1, tiled=True)]
    all_to_all x2 -> x0, waiting for transfers between devices: 13.6 us -> none  [the longest x1 13.6 us: heads_attention(): lax.all_to_all(queries, 'help', split_axis=1, concat_axis=0, tiled=True)]
    all_to_all x2 -> x0, starting transfers between devices: 8.78 us -> none  [the longest x1 5.16 us: heads_attention(): lax.all_to_all(queries, 'help', split_axis=1, concat_axis=0, tiled=True)]
    another operation x3 -> x0, loops' own time: 8.36 us -> none  [the longest x1 8.23 us: heads_attention(): row_output = lax.map(one_block, jnp.arange(query_blocks, dtype=jnp.int32))]
  transfers between devices with their start and end apart: 3 -> 0, of which waited for: 2 -> 0; matrix products, arithmetic and copies ran while one was open for 28% -> 0% of each run, Pallas kernels for 0% -> 0%
where the time goes in v1:
time: 97.2 us; the launch traced here: 97 us
  Pallas kernels  86.7 us (89%)
  local copies, waits for them, and re-layouts  10.2 us (10%)
    pallas_call x1, Pallas kernels, on_device(): pl.pallas_call(functools.partial(kernel, dims), out_shape=jax.ShapeDtypeS...  86.7 us
    unnamed x3, local copies, waits for them, and re-layouts  7.5 us

profile of v1, /device:TPU:0, one launch (start us, length us, event | category | flops | bytes accessed | tf_op | source)
XLA Modules:
  0.0 97.0 jit_solution(6128074190447796950)
XLA Ops:
  0.0 1.3 %broadcast_in_dim.8.segr_ref = s32[8,256]{1,0:T(8,128)} broadcast(s32[256]{0:T(256)} %bitcast.10), dimensions={1} | broadcast | bytes 9216 | tf_op jit(solution)/shard_map/broadcast_in_dim | solution.py:428
  1.3 1.5 %copy.10.segc_ref = s32[256,1]{1,0:T(8,128)} copy(s32[256,1]{0,1:T(1,128)} %bitcast.11) | data formatting | bytes 2048 | tf_op jit(solution)/shard_map/broadcast_in_dim;reshape | solution.py:429
  2.7 1.9 %copy.14 = bf16[256,4,256]{2,0,1:T(8,128)(2,1)} copy(bf16[256,4,256]{2,1,0:T(4,128)(2,1)} %param.6) | data formatting | bytes 1048576 | tf_op args[1]
  4.6 2.5 %copy.13 = bf16[256,16,128]{2,0,1:T(8,128)(2,1)} copy(bf16[256,16,128]{2,1,0:T(8,128)(2,1)} %param.5) | data formatting | bytes 2097152 | tf_op args[0]
  7.1 86.7 %shard_map.55 = bf16[256,4096]{1,0:T(8,128)(2,1)} custom-call(bf16[16,256,128]{2,1,0:T(8,128)(2,1)} %bitcast.8, bf16[4,256,256]{2,1,0:T(8,128)(2,1)} %bitcast.9, s32[8,256]{1,0:T(8,128)} %broadcast_in_dim.8.segr_ref, s32[256,1]{1,0:T(8,128)} %copy.10.segc_ref, bf16[256,4096]{1,0:T(8,128)(2,1)} %res_ref.1, bf16[2048,512]{1,0:T(8,128)(2,1)} %w_ref.1), custom_call_target="tpu_custom_call" | custom-call | flops 6000000000 | bytes 20000000 | tf_op jit(solution)/shard_map/pallas_call | solution.py:392
  93.8 3.1 %copy.16 = bf16[256,4096]{1,0:T(8,128)(2,1)} copy(bf16[256,4096]{1,0:T(8,128)(2,1)} %shard_map.55) | data formatting | bytes 4194304

commit v2 on v1

--- a/solution.py
+++ b/solution.py
@@ -16,14 +16,15 @@
     dims,
     q_ref,
     kv_ref,
-    segr_ref,
-    segc_ref,
+    seg_ref,
     res_ref,
     w_ref,
     out_ref,
     wbuf,
     kvbuf,
     segbuf,
+    segcol,
+    qraw,
     qbuf,
     att,
     resbuf,
@@ -33,6 +34,7 @@
     p_send,
     kv_recv,
     kv_send,
+    relay_send,
     seg_recv,
     seg_send,
     res_recv,
@@ -44,10 +46,11 @@
     loc,
     loc_out,
 ):
-    nz, ny, nx, back, heads, heads_kv, hd, rows, cols, width = dims
+    nz, ny, nx, back, heads, heads_kv, hd, rows, cols, width, direct, relays = dims
     nh = ny * nx
-    quarter = width // nh
-    piece_rows = quarter // 2
+    quarter = (width - direct) // nh
+    split = quarter // 32 * 16
+    sizes = (split, quarter - split, direct)
     dp = lax.axis_index("dp")
     h = lax.axis_index("help")
     z, c = dp // 2, lax.rem(dp, 2)
@@ -63,8 +66,13 @@
         return pl.ds(pl.multiple_of(core * rows, rows), rows)
 
     def piece(zp, hp, half):
-        start = pl.multiple_of(hp * quarter + half * piece_rows, piece_rows)
-        return wbuf.at[zp, pl.ds(start, piece_rows)]
+        if half == 2:
+            return wbuf.at[zp, 0:direct]
+        start = pl.multiple_of(direct + hp * quarter + half * split, 16)
+        return wbuf.at[zp, pl.ds(start, sizes[half])]
+
+    def w_sem(zp, hp, half):
+        return w_recv.at[zp, nh, 0] if half == 2 else w_recv.at[zp, hp, half]
 
     def remote(src, dst, ssem, rsem, dev):
         return pltpu.make_async_remote_copy(
@@ -91,47 +99,68 @@
 
     def z_copy(src, zp, half, way, step):
         dev = (dp + 2, h) if way == 0 else (dp - 2, h)
-        return remote(src, piece(zp, h, half), z_send.at[way, step, half], w_recv.at[zp, h, half], dev)
+        return remote(src, piece(zp, h, half), z_send.at[way, step, half], w_sem(zp, h, half), dev)
 
     def own_piece(half):
-        start = pl.multiple_of(h * quarter + half * piece_rows, piece_rows)
-        return w_ref.at[pl.ds(start, piece_rows)]
-
-    for half in range(2):
-
+        if half == 2:
+            return w_ref.at[0:direct]
+        start = pl.multiple_of(direct + h * quarter + half * split, 16)
+        return w_ref.at[pl.ds(start, sizes[half])]
+
+    def own_out(half):
         @pl.when(z < nz - 1)
-        def _(half=half):
+        def _():
             z_copy(own_piece(half), z, half, 0, 0).start()
 
         @pl.when(z > 0)
-        def _(half=half):
+        def _():
             z_copy(own_piece(half), z, half, 1, 0).start()
 
+    own_out(0)
+    own_out(1)
+
     def seg_copy(j):
-        return remote(segr_ref, segbuf.at[j], seg_send.at[j], seg_recv.at[j], (dp, lax.rem(h + j, nh)))
+        return remote(segbuf.at[0], segbuf.at[j], seg_send.at[j], seg_recv.at[j], (dp, lax.rem(h + j, nh)))
 
     def kv_copy(j, g):
         return remote(
             kv_ref.at[g], kvbuf.at[j, g], kv_send.at[j, g], kv_recv.at[j, g], (dp, lax.rem(h + j, nh))
         )
 
+    def beside(j):
+        if j % nx == 0:
+            return h + j < nh
+        return x + j < nx
+
+    def relay_copy(i, g):
+        j, t = relays[i]
+        return remote(
+            kvbuf.at[j, g], kvbuf.at[j + t, g], relay_send.at[i, g], kv_recv.at[j + t, g], (dp, lax.rem(h + t + nh, nh))
+        )
+
+    def relaying(i):
+        j, t = relays[i]
+        return (h >= j) & (x + t >= 0) & (x + t < nx)
+
+    for g in range(heads_kv):
+        for j in range(1, back + 1):
+
+            @pl.when(beside(j))
+            def _(j=j, g=g):
+                kv_copy(j, g).start()
+
+    segbuf[0] = jnp.broadcast_to(seg_ref[...], (8, rows))
     for j in range(1, back + 1):
 
         @pl.when(h + j < nh)
         def _(j=j):
             seg_copy(j).start()
 
-    for g in range(heads_kv):
-        for j in range(1, back + 1):
-
-            @pl.when(h + j < nh)
-            def _(j=j, g=g):
-                kv_copy(j, g).start()
+    segcol[...] = jnp.transpose(jnp.broadcast_to(seg_ref[...], (128, rows)))
 
     local = [
-        pltpu.make_async_copy(q_ref, qbuf, loc.at[0]),
+        pltpu.make_async_copy(q_ref, qraw, loc.at[0]),
         pltpu.make_async_copy(kv_ref, kvbuf.at[0], loc.at[1]),
-        pltpu.make_async_copy(segr_ref, segbuf.at[0], loc.at[2]),
         pltpu.make_async_copy(w_ref, wbuf.at[z], loc.at[3]),
     ]
     for copy in local:
@@ -167,18 +196,18 @@
     def to_x(zp, hp, half):
         for xm in x_mates:
             remote(
-                piece(zp, hp, half), piece(zp, hp, half), p_send.at[zp], w_recv.at[zp, hp, half], (dp, y * nx + xm)
+                piece(zp, hp, half), piece(zp, hp, half), p_send.at[zp], w_sem(zp, hp, half), (dp, y * nx + xm)
             ).start()
 
     def to_y(zp, hp, half):
         for ym in y_mates:
             remote(
-                piece(zp, hp, half), piece(zp, hp, half), p_send.at[zp], w_recv.at[zp, hp, half], (dp, ym * nx + x)
+                piece(zp, hp, half), piece(zp, hp, half), p_send.at[zp], w_sem(zp, hp, half), (dp, ym * nx + x)
             ).start()
 
     def arrived(zp, hp, half):
         remote(
-            piece(zp, hp, half), piece(zp, hp, half), p_send.at[zp], w_recv.at[zp, hp, half], sib
+            piece(zp, hp, half), piece(zp, hp, half), p_send.at[zp], w_sem(zp, hp, half), sib
         ).wait_recv()
 
     def from_z(step, half):
@@ -189,8 +218,9 @@
             def _():
                 z_copy(piece(zp, h, half), zp, half, way, step).start()
 
-            to_x(zp, h, half)
-            to_y(zp, h, half)
+            if half < 2:
+                to_x(zp, h, half)
+                to_y(zp, h, half)
 
         both_ways(step, run)
 
@@ -209,17 +239,26 @@
     group = heads // heads_kv
     per_chunk = 2
 
+    def fetch(g):
+        for j in range(back, 0, -1):
+
+            @pl.when(h >= j)
+            def _(j=j):
+                if g == 0:
+                    seg_copy(j).wait_recv()
+                kv_copy(j, g).wait_recv()
+
+            for i, (held, _) in enumerate(relays):
+                if held == j:
+
+                    @pl.when(relaying(i))
+                    def _(i=i):
+                        relay_copy(i, g).start()
+
     def attend(g, first):
-        if first == 0:
-            for j in range(1, back + 1):
-
-                @pl.when(h >= j)
-                def _(j=j):
-                    if g == 0:
-                        seg_copy(j).wait_recv()
-                    kv_copy(j, g).wait_recv()
-
-        q_seg = segc_ref[...]
+        if first + per_chunk >= group and g + 1 < heads_kv:
+            fetch(g + 1)
+        q_seg = segcol[:, 0:1]
         here = [g * group + first + i for i in range(per_chunk)]
 
         def scores(head, j, allowed):
@@ -295,8 +334,10 @@
                 arrived(zp, ym * nx + xm, 0)
                 arrived(zp, ym * nx + xm, 1)
 
-    for copy in local[:3]:
+    for copy in local[:2]:
         copy.wait()
+    qbuf[...] = jnp.transpose(qraw[...], (1, 0, 2))
+    fetch(0)
     work = [
         functools.partial(attend, g, first)
         for g in range(heads_kv)
@@ -313,13 +354,17 @@
         from_z(step, 0)
         compute(1)
         from_z(step, 1)
+        if step == 1:
+            own_out(2)
+        else:
+            from_z(step - 1, 2)
         compute(1)
         relay(step)
         compute(2)
         if step == 2 or nz <= 2:
             compute(len(work))
             att_copy(c).start()
-            local[3].wait()
+            local[2].wait()
             for zp in range(nz):
                 res_local(zp).wait()
                 res_copy(zp).wait_recv()
@@ -327,6 +372,8 @@
             project(z, 0)
 
     for step in range(1, nz):
+        if step == nz - 1:
+            from_z(step, 2)
 
         def run(zp, way):
             complete(zp)
@@ -345,10 +392,20 @@
         @pl.when(h + j < nh)
         def _(j=j):
             seg_copy(j).wait_send()
+
+        @pl.when(beside(j))
+        def _(j=j):
             for g in range(heads_kv):
                 kv_copy(j, g).wait_send()
 
-    for half in range(2):
+    for i in range(len(relays)):
+
+        @pl.when(relaying(i))
+        def _(i=i):
+            for g in range(heads_kv):
+                relay_copy(i, g).wait_send()
+
+    for half in range(3):
 
         @pl.when(z < nz - 1)
         def _(half=half):
@@ -361,7 +418,7 @@
     for step in range(1, nz):
 
         def drain(zp, way):
-            for half in range(2):
+            for half in range(3):
 
                 @pl.when((z < nz - 1) if way == 0 else (z > 0))
                 def _(half=half):
@@ -384,29 +441,41 @@
         nx -= 1
     ny = nh // nx
     back = nh // 2
-    dims = (nz, ny, nx, back, heads, heads_kv, hd, rows, cols, width)
-    seg = segment_ids.reshape(rows)
+    direct = 0
+    for part in (width // 8, 3 * width // 16):
+        if (width - part) % (16 * nh) == 0:
+            direct = part
+    relays = tuple(
+        (j, t)
+        for j in range(nx, back + 1, nx)
+        for t in range(1 - nx, nx)
+        if t and 1 <= j + t <= back
+    )
+    dims = (nz, ny, nx, back, heads, heads_kv, hd, rows, cols, width, direct, relays)
     any_spec = pl.BlockSpec(memory_space=pl.ANY)
     dma = pltpu.SemaphoreType.DMA
     bf16 = jnp.bfloat16
     return pl.pallas_call(
         functools.partial(kernel, dims),
         out_shape=jax.ShapeDtypeStruct(residual.shape, bf16),
-        in_specs=[any_spec, any_spec, any_spec, pl.BlockSpec(memory_space=pltpu.VMEM), any_spec, any_spec],
+        in_specs=[any_spec, any_spec, pl.BlockSpec(memory_space=pltpu.VMEM), any_spec, any_spec],
         out_specs=any_spec,
         scratch_shapes=[
             pltpu.VMEM((nz, width, cols), bf16),
             pltpu.VMEM((back + 1, heads_kv, rows, 2 * hd), bf16),
             pltpu.VMEM((back + 1, 8, rows), jnp.int32),
+            pltpu.VMEM((rows, 128), jnp.int32),
+            pltpu.VMEM((rows, heads, hd), bf16),
             pltpu.VMEM((heads, rows, hd), bf16),
             pltpu.VMEM((2 * rows, width), bf16),
             pltpu.VMEM((nz, 2 * rows, cols), bf16),
             pltpu.VMEM((nz, 2 * rows, cols), bf16),
-            dma((nz, nh, 2)),
-            dma((2, nz, 2)),
+            dma((nz, nh + 1, 2)),
+            dma((2, nz, 3)),
             dma((nz,)),
             dma((back + 1, heads_kv)),
             dma((back + 1, heads_kv)),
+            dma((max(1, len(relays)), heads_kv)),
             dma((back + 1,)),
             dma((back + 1,)),
             dma((nz,)),
@@ -423,10 +492,9 @@
         ),
         cost_estimate=pl.CostEstimate(flops=6 * 10**9, bytes_accessed=2 * 10**7, transcendentals=3 * 10**6),
     )(
-        jnp.transpose(queries, (1, 0, 2)),
+        queries,
         jnp.transpose(keys_values, (1, 0, 2)),
-        jnp.broadcast_to(seg[None, :], (8, rows)),
-        seg[:, None],
+        segment_ids,
         residual,
         out_weight,
     )

time: 97.2 us -> 94.9 us (0.976)
  local copies, waits for them, and re-layouts: 10.2 us -> 5.03 us
  Pallas kernels: 86.7 us -> 89.7 us
    pallas_call x1, Pallas kernels: 86.7 us -> 89.7 us  [on_device(): pl.pallas_call(functools.partial(kernel, dims), out_shape=jax.ShapeDtypeS...]
    unnamed x3 -> x2, local copies, waits for them, and re-layouts: 7.5 us -> 5.03 us
    another operation x1 -> x0, local copies, waits for them, and re-layouts: 1.46 us -> none  [on_device(): seg[:, None]]
    broadcast_in_dim x1 -> x0, local copies, waits for them, and re-layouts: 1.27 us -> none  [on_device(): jnp.broadcast_to(seg[None, :], (8, rows))]
where the time goes in v2:
time: 94.9 us; the launch traced here: 94.7 us
  Pallas kernels  89.7 us (95%)
  local copies, waits for them, and re-layouts  5.03 us (5%)
    pallas_call x1, Pallas kernels, on_device(): pl.pallas_call(functools.partial(kernel, dims), out_shape=jax.ShapeDtypeS...  89.7 us
    unnamed x2, local copies, waits for them, and re-layouts  5.03 us

profile of v2, /device:TPU:0, one launch (start us, length us, event | category | flops | bytes accessed | tf_op | source)
XLA Modules:
  0.0 94.7 jit_solution(5914209130181407263)
XLA Ops:
  0.0 1.9 %copy.8 = bf16[256,4,256]{2,0,1:T(8,128)(2,1)} copy(bf16[256,4,256]{2,1,0:T(4,128)(2,1)} %param.6) | data formatting | bytes 1048576 | tf_op args[1]
  1.9 89.7 %shard_map.55 = bf16[256,4096]{1,0:T(8,128)(2,1)} custom-call(bf16[256,16,128]{2,1,0:T(8,128)(2,1)} %q_ref.1, bf16[4,256,256]{2,1,0:T(8,128)(2,1)} %bitcast.3, s32[1,256]{1,0:T(1,128)} %seg_ref.1, bf16[256,4096]{1,0:T(8,128)(2,1)} %res_ref.1, bf16[2048,512]{1,0:T(8,128)(2,1)} %w_ref.1), custom_call_target="tpu_custom_call" | custom-call | flops 6000000000 | bytes 20000000 | tf_op jit(solution)/shard_map/pallas_call | solution.py:458
  91.6 3.1 %copy.10 = bf16[256,4096]{1,0:T(8,128)(2,1)} copy(bf16[256,4096]{1,0:T(8,128)(2,1)} %shard_map.55) | data formatting | bytes 4194304

commit v3 on v2

--- a/solution.py
+++ b/solution.py
@@ -156,7 +156,7 @@
         def _(j=j):
             seg_copy(j).start()
 
-    segcol[...] = jnp.transpose(jnp.broadcast_to(seg_ref[...], (128, rows)))
+    segcol[0] = jnp.transpose(jnp.broadcast_to(seg_ref[...], (rows, rows)))
 
     local = [
         pltpu.make_async_copy(q_ref, qraw, loc.at[0]),
@@ -235,7 +235,7 @@
 
         both_ways(step, run)
 
-    scale = 1.0 / math.sqrt(hd)
+    scale = math.log2(math.e) / math.sqrt(hd)
     group = heads // heads_kv
     per_chunk = 2
 
@@ -246,6 +246,7 @@
             def _(j=j):
                 if g == 0:
                     seg_copy(j).wait_recv()
+                    segcol[j] = jnp.transpose(jnp.broadcast_to(segbuf[j, 0:1, :], (rows, rows)))
                 kv_copy(j, g).wait_recv()
 
             for i, (held, _) in enumerate(relays):
@@ -258,46 +259,46 @@
     def attend(g, first):
         if first + per_chunk >= group and g + 1 < heads_kv:
             fetch(g + 1)
-        q_seg = segcol[:, 0:1]
+        q_seg = seg_ref[...]
         here = [g * group + first + i for i in range(per_chunk)]
 
         def scores(head, j, allowed):
             s = lax.dot_general(
-                qbuf[head], kvbuf[j, g, :, 0:hd], (((1,), (1,)), ((), ())), preferred_element_type=jnp.float32
+                kvbuf[j, g, :, 0:hd], qbuf[head], (((1,), (1,)), ((), ())), preferred_element_type=jnp.float32
             )
             return jnp.where(allowed, s * scale, masked_score)
 
-        def mix(weights, j):
-            return jnp.dot(
-                weights.astype(jnp.bfloat16), kvbuf[j, g, :, hd:], preferred_element_type=jnp.float32
-            )
-
-        same = q_seg == segbuf[0, 0:1, :]
-        causal = lax.broadcasted_iota(jnp.int32, (rows, rows), 1) <= lax.broadcasted_iota(
-            jnp.int32, (rows, rows), 0
-        )
+        def mix(values, weights):
+            return jnp.dot(values, weights.astype(jnp.bfloat16), preferred_element_type=jnp.float32)
+
+        causal = lax.broadcasted_iota(jnp.int32, (rows, rows), 0) <= lax.broadcasted_iota(
+            jnp.int32, (rows, rows), 1
+        )
+        own = (segcol[0] == q_seg) & causal
+        values = jnp.transpose(kvbuf[0, g, :, hd:])
         states = []
         for head in here:
-            s = scores(head, 0, same & causal)
-            top = jnp.max(s, axis=-1, keepdims=True)
-            weights = jnp.exp(s - top)
-            states.append((top, jnp.sum(weights, axis=-1, keepdims=True), mix(weights, 0)))
+            s = scores(head, 0, own)
+            top = jnp.max(s, axis=0, keepdims=True)
+            weights = jnp.exp2(s - top)
+            states.append((top, jnp.sum(weights, axis=0, keepdims=True), mix(values, weights)))
 
         def earlier(j, states):
-            allowed = q_seg == segbuf[j, 0:1, :]
+            allowed = segcol[j] == q_seg
+            values = jnp.transpose(kvbuf[j, g, :, hd:])
             after = []
             for head, (top, total, running) in zip(here, states):
                 s = scores(head, j, allowed)
-                new_top = jnp.maximum(top, jnp.max(s, axis=-1, keepdims=True))
-                weights = jnp.exp(s - new_top)
-                factor = jnp.exp(top - new_top)
-                total = total * factor + jnp.sum(weights, axis=-1, keepdims=True)
-                after.append((new_top, total, running * factor + mix(weights, j)))
+                new_top = jnp.maximum(top, jnp.max(s, axis=0, keepdims=True))
+                weights = jnp.exp2(s - new_top)
+                factor = jnp.exp2(top - new_top)
+                total = total * factor + jnp.sum(weights, axis=0, keepdims=True)
+                after.append((new_top, total, running * factor + mix(values, weights)))
             return tuple(after)
 
         states = lax.fori_loop(1, jnp.minimum(h, back) + 1, earlier, tuple(states))
         for head, (top, total, running) in zip(here, states):
-            att[own_rows(c), head * hd : (head + 1) * hd] = (running / total).astype(jnp.bfloat16)
+            att[own_rows(c), head * hd : (head + 1) * hd] = jnp.transpose(running / total).astype(jnp.bfloat16)
 
     def att_copy(core):
         return remote(att.at[own_rows(core)], att.at[own_rows(core)], att_send, att_recv, sib)
@@ -354,22 +355,28 @@
         from_z(step, 0)
         compute(1)
         from_z(step, 1)
-        if step == 1:
+        compute(1)
+        if step == 2:
             own_out(2)
-        else:
-            from_z(step - 1, 2)
+        if step > 1:
+            relay(step - 1)
+        if step > 2:
+            from_z(step - 2, 2)
         compute(1)
-        relay(step)
-        compute(2)
-        if step == 2 or nz <= 2:
-            compute(len(work))
-            att_copy(c).start()
-            local[2].wait()
-            for zp in range(nz):
-                res_local(zp).wait()
-                res_copy(zp).wait_recv()
-            att_copy(1 - c).wait_recv()
-            project(z, 0)
+    if nz == 2:
+        own_out(2)
+    compute(len(work))
+    att_copy(c).start()
+    for copy in local[2:]:
+        copy.wait()
+    for zp in range(nz):
+        res_local(zp).wait()
+        res_copy(zp).wait_recv()
+    if nz > 2:
+        from_z(nz - 2, 2)
+    relay(nz - 1)
+    att_copy(1 - c).wait_recv()
+    project(z, 0)
 
     for step in range(1, nz):
         if step == nz - 1:
@@ -464,7 +471,7 @@
             pltpu.VMEM((nz, width, cols), bf16),
             pltpu.VMEM((back + 1, heads_kv, rows, 2 * hd), bf16),
             pltpu.VMEM((back + 1, 8, rows), jnp.int32),
-            pltpu.VMEM((rows, 128), jnp.int32),
+            pltpu.VMEM((back + 1, rows, rows), jnp.int32),
             pltpu.VMEM((rows, heads, hd), bf16),
             pltpu.VMEM((heads, rows, hd), bf16),
             pltpu.VMEM((2 * rows, width), bf16),

time: 94.9 us -> 94.4 us (level)
  no operation moved by 1% of the time
where the time goes in v3:
time: 94.4 us; the launch traced here: 94.2 us
  Pallas kernels  89.2 us (94%)
  local copies, waits for them, and re-layouts  5.03 us (5%)
    pallas_call x1, Pallas kernels, on_device(): pl.pallas_call(functools.partial(kernel, dims), out_shape=jax.ShapeDtypeS...  89.2 us
    unnamed x2, local copies, waits for them, and re-layouts  5.03 us

profile of v3, /device:TPU:0, one launch (start us, length us, event | category | flops | bytes accessed | tf_op | source)
XLA Modules:
  0.0 94.2 jit_solution(10007763390742096635)
XLA Ops:
  0.0 1.9 %copy.8 = bf16[256,4,256]{2,0,1:T(8,128)(2,1)} copy(bf16[256,4,256]{2,1,0:T(4,128)(2,1)} %param.6) | data formatting | bytes 1048576 | tf_op args[1]
  1.9 89.2 %shard_map.55 = bf16[256,4096]{1,0:T(8,128)(2,1)} custom-call(bf16[256,16,128]{2,1,0:T(8,128)(2,1)} %q_ref.1, bf16[4,256,256]{2,1,0:T(8,128)(2,1)} %bitcast.3, s32[1,256]{1,0:T(1,128)} %seg_ref.1, bf16[256,4096]{1,0:T(8,128)(2,1)} %res_ref.1, bf16[2048,512]{1,0:T(8,128)(2,1)} %w_ref.1), custom_call_target="tpu_custom_call" | custom-call | flops 6000000000 | bytes 20000000 | tf_op jit(solution)/shard_map/pallas_call | solution.py:465
  91.1 3.1 %copy.10 = bf16[256,4096]{1,0:T(8,128)(2,1)} copy(bf16[256,4096]{1,0:T(8,128)(2,1)} %shard_map.55) | data formatting | bytes 4194304

commit v4 on v3

--- a/solution.py
+++ b/solution.py
@@ -356,15 +356,12 @@
         compute(1)
         from_z(step, 1)
         compute(1)
-        if step == 2:
+        if step == 1:
             own_out(2)
-        if step > 1:
+        else:
+            from_z(step - 1, 2)
             relay(step - 1)
-        if step > 2:
-            from_z(step - 2, 2)
         compute(1)
-    if nz == 2:
-        own_out(2)
     compute(len(work))
     att_copy(c).start()
     for copy in local[2:]:
@@ -372,8 +369,6 @@
     for zp in range(nz):
         res_local(zp).wait()
         res_copy(zp).wait_recv()
-    if nz > 2:
-        from_z(nz - 2, 2)
     relay(nz - 1)
     att_copy(1 - c).wait_recv()
     project(z, 0)
@@ -448,10 +443,7 @@
         nx -= 1
     ny = nh // nx
     back = nh // 2
-    direct = 0
-    for part in (width // 8, 3 * width // 16):
-        if (width - part) % (16 * nh) == 0:
-            direct = part
+    direct = width // 8
     relays = tuple(
         (j, t)
         for j in range(nx, back + 1, nx)

time: 94.4 us -> 86.8 us (0.919)
  Pallas kernels: 89.2 us -> 81.6 us
    pallas_call x1, Pallas kernels: 89.2 us -> 81.6 us  [on_device(): pl.pallas_call(functools.partial(kernel, dims), out_shape=jax.ShapeDtypeS...]
where the time goes in v4:
time: 86.8 us; the launch traced here: 86.6 us
  Pallas kernels  81.6 us (94%)
  local copies, waits for them, and re-layouts  5.03 us (6%)
    pallas_call x1, Pallas kernels, on_device(): pl.pallas_call(functools.partial(kernel, dims), out_shape=jax.ShapeDtypeS...  81.6 us
    unnamed x2, local copies, waits for them, and re-layouts  5.03 us

profile of v4, /device:TPU:0, one launch (start us, length us, event | category | flops | bytes accessed | tf_op | source)
XLA Modules:
  0.0 86.6 jit_solution(8565711041848410295)
XLA Ops:
  0.0 1.9 %copy.8 = bf16[256,4,256]{2,0,1:T(8,128)(2,1)} copy(bf16[256,4,256]{2,1,0:T(4,128)(2,1)} %param.6) | data formatting | bytes 1048576 | tf_op args[1]
  1.9 81.6 %shard_map.55 = bf16[256,4096]{1,0:T(8,128)(2,1)} custom-call(bf16[256,16,128]{2,1,0:T(8,128)(2,1)} %q_ref.1, bf16[4,256,256]{2,1,0:T(8,128)(2,1)} %bitcast.3, s32[1,256]{1,0:T(1,128)} %seg_ref.1, bf16[256,4096]{1,0:T(8,128)(2,1)} %res_ref.1, bf16[2048,512]{1,0:T(8,128)(2,1)} %w_ref.1), custom_call_target="tpu_custom_call" | custom-call | flops 6000000000 | bytes 20000000 | tf_op jit(solution)/shard_map/pallas_call | solution.py:457
  83.5 3.1 %copy.10 = bf16[256,4096]{1,0:T(8,128)(2,1)} copy(bf16[256,4096]{1,0:T(8,128)(2,1)} %shard_map.55) | data formatting | bytes 4194304
